TPU v7x, 32 devices: a whole 2x2x4 slice. The times are simulated.
32 devices in a mesh: slab: 16 (over z, y, x), graph: 2 (over core).
Axes of the slice: x: 2, y: 2, z: 4, core: 2. Of those that a mesh axis runs over, the one named last changes fastest.
Arguments:
- nodes: bfloat16 [16384, 9, 128], P(('slab', 'graph')), may hold values from -6 to 6
- boundary: int32 [16, 2, 640], P('slab'), may hold values from 0 to 1023
- sources: int32 [81920], P(('slab', 'graph')), may hold values from 0 to 2303
- targets: int32 [81920], P(('slab', 'graph')), may hold values from 0 to 1023
- block_counts: int32 [16, 2], replicated, may hold values from 10 to 20, as said below
- wigner: float32 [35, 81920], P(None, ('slab', 'graph')), may hold values from -3 to 3
- radial: bfloat16 [81920, 128], P(('slab', 'graph')), may hold values from -6 to 6
- w_zero: bfloat16 [384, 384], replicated, may hold values from -0.3125 to 0.3125
- w_one: bfloat16 [2, 256, 256], replicated, may hold values from -0.25 to 0.25
- w_two: bfloat16 [2, 128, 128], replicated, may hold values from -0.375 to 0.375
Outputs:
- updated: bfloat16 [16384, 9, 128], P(('slab', 'graph'))
Inputs may be any that keep to these rules, and one draw needn't show every extreme that they name: Slots of device (s, g) from block_counts[s, g] * 128 on are padding; every draw has some device with 20 live blocks.
All inputs are finite; a program needn't handle non-finite values.
Results may differ from a plain program's by a relative error of at most 0.0064.
Values may be sent and summed in bfloat16 or wider, within the bound.
No kernel may reach another device: no remote copies, remote signals or barrier semaphores. Data moves between devices by JAX's collectives and lax.ppermute only.
A program may use at most 64 MiB of HBM per device.

v0:
```python
import jax
import jax.numpy as jnp
from jax import lax
from jax.sharding import PartitionSpec as P

EDGE_BLOCK = 128
GROUP_BLOCKS = 4


message_scale = 0.2
wigner_blocks = ((0, 0, 1), (1, 1, 3), (10, 4, 5))


def shifted(x, axis, by):
    size = lax.axis_size(axis)
    return lax.ppermute(x, axis, [(i, (i + by) % size) for i in range(size)])


def rotate(coeffs, wig_rows, inverse):
    out_list = []
    for offset, first_coef, block_size in wigner_blocks:
        for row_index in range(block_size):
            summed = None
            for col_index in range(block_size):
                if inverse:
                    entry_index = offset + col_index * block_size + row_index
                else:
                    entry_index = offset + row_index * block_size + col_index
                product_term = wig_rows[entry_index][:, None] * coeffs[:, first_coef + col_index, :]
                summed = product_term if summed is None else summed + product_term
            out_list.append(summed)
    return jnp.stack(out_list, axis=1)


def build_pair(pair_weights):
    real_part = pair_weights[0]
    imag_part = pair_weights[1]
    top_half = jnp.concatenate([real_part, imag_part], axis=1)
    low_half = jnp.concatenate([-imag_part, real_part], axis=1)
    return jnp.concatenate([top_half, low_half], axis=0)


def mix_orders(rotated, w_zero, pair_one, pair_two):
    chan = rotated.shape[2]
    zero_in = jnp.concatenate([rotated[:, 0], rotated[:, 2], rotated[:, 6]], axis=1)
    zero_out = jnp.dot(zero_in, w_zero, preferred_element_type=jnp.float32)
    one_in = jnp.concatenate([rotated[:, 3], rotated[:, 7], rotated[:, 1], rotated[:, 5]], axis=1)
    one_out = jnp.dot(one_in, pair_one, preferred_element_type=jnp.float32)
    two_in = jnp.concatenate([rotated[:, 8], rotated[:, 4]], axis=1)
    two_out = jnp.dot(two_in, pair_two, preferred_element_type=jnp.float32)
    pieces = [
        zero_out[:, :chan],
        one_out[:, 2 * chan : 3 * chan],
        zero_out[:, chan : 2 * chan],
        one_out[:, :chan],
        two_out[:, chan:],
        one_out[:, 3 * chan :],
        zero_out[:, 2 * chan :],
        one_out[:, chan : 2 * chan],
        two_out[:, :chan],
    ]
    return jnp.stack(pieces, axis=1).astype(jnp.bfloat16)


def front(src_rows, wig_rows, rad_rows):
    turned = rotate(src_rows.astype(jnp.float32), wig_rows, False)
    return (turned * rad_rows.astype(jnp.float32)[:, None, :]).astype(jnp.bfloat16)


def finish(mixed, wig_rows, live_mask):
    turned = rotate(mixed.astype(jnp.float32), wig_rows, True)
    return (turned * live_mask[:, None, None]).astype(jnp.bfloat16)


def scatter_rows(partial_value, messages, tgt_rows):
    slab_atoms = partial_value.shape[0]
    onehot = (tgt_rows[:, None] == jnp.arange(slab_atoms, dtype=jnp.int32)[None, :]).astype(
        jnp.bfloat16
    )
    flat = messages.reshape(messages.shape[0], -1)
    return partial_value + lax.dot_general(
        onehot, flat, (((0,), (0,)), ((), ())), preferred_element_type=jnp.float32
    )


def accumulate(partial_value, base, live_edges, make_mixed, targets, wigner):
    group_rows = GROUP_BLOCKS * EDGE_BLOCK
    positions = jnp.arange(group_rows, dtype=jnp.int32)

    def one_group(group_index, carried):
        offset = base + group_index * group_rows
        wig_rows = lax.dynamic_slice_in_dim(wigner, offset, group_rows, 1)
        tgt_rows = lax.dynamic_slice_in_dim(targets, offset, group_rows, 0)
        live_mask = (group_index * group_rows + positions < live_edges).astype(jnp.float32)
        messages = finish(make_mixed(offset, wig_rows), wig_rows, live_mask)
        return scatter_rows(carried, messages, tgt_rows)

    group_count = (live_edges + group_rows - 1) // group_rows
    return lax.fori_loop(0, group_count, one_group, partial_value)


def per_device(
    nodes, boundary, sources, targets, block_counts, wigner, radial, w_zero, w_one, w_two
):
    pair_one = build_pair(w_one)
    pair_two = build_pair(w_two)
    group_rows = GROUP_BLOCKS * EDGE_BLOCK
    slab_rows = lax.all_gather(nodes, "graph", axis=0, tiled=True)
    upper_rows = jnp.take(slab_rows, boundary[0, 1], axis=0)
    lower_rows = jnp.take(slab_rows, boundary[0, 0], axis=0)
    from_below = shifted(upper_rows, "slab", 1)
    from_above = shifted(lower_rows, "slab", -1)
    lookup = jnp.concatenate([slab_rows, from_below, from_above], axis=0)
    slab_index = lax.axis_index("slab")
    graph_index = lax.axis_index("graph")
    own_edges = block_counts[slab_index, graph_index] * EDGE_BLOCK

    def local_mixed(offset, wig_rows):
        src_index = lax.dynamic_slice_in_dim(sources, offset, group_rows, 0)
        rad_rows = lax.dynamic_slice_in_dim(radial, offset, group_rows, 0)
        turned = front(jnp.take(lookup, src_index, axis=0), wig_rows, rad_rows)
        return mix_orders(turned, w_zero, pair_one, pair_two)

    partial_value = jnp.zeros((slab_rows.shape[0], 9 * nodes.shape[2]), jnp.float32)
    partial_value = accumulate(partial_value, 0, own_edges, local_mixed, targets, wigner)
    summed = lax.psum_scatter(partial_value, "graph", scatter_dimension=0, tiled=True)
    return (summed * message_scale).astype(jnp.bfloat16).reshape(nodes.shape)


def solution(mesh):
    return jax.shard_map(
        per_device,
        mesh=mesh,
        in_specs=(
            P(("slab", "graph"), None, None),
            P("slab", None, None),
            P(("slab", "graph")),
            P(("slab", "graph")),
            P(),
            P(None, ("slab", "graph")),
            P(("slab", "graph"), None),
            P(),
            P(),
            P(),
        ),
        out_specs=P(("slab", "graph"), None, None),
        check_vma=False,
    )
```

profile of v0, /device:TPU:0, one launch (start us, length us, event | category | flops | bytes accessed | tf_op | source)
XLA Modules:
  0.0 320.6 jit_solution(3195264407654729008)
XLA Ops:
  8.1 14.5 %all-gather.2.cloned.1.call-done = bf16[1024,9,128]{2,0,1:T(8,128)(2,1)} async-done(((bf16[512,9,128]{2,0,1:T(8,128)(2,1)}), bf16[1024,9,128]{2,0,1:T(8,128)(2,1)}) %all-gather.2.cloned.1.call-update) | async-done | bytes 2359312 | tf_op jit(solution)/shard_map/all_gather | solution.py:108
  22.6 5.4 %copy.24 = bf16[1024,9,128]{2,1,0:T(8,128)(2,1)} copy(bf16[1024,9,128]{2,0,1:T(8,128)(2,1)} %all-gather.2.cloned.1.call-done) | data formatting | bytes 4718592 | tf_op jit(solution)/shard_map/all_gather | solution.py:108
  28.0 3.5 %gather_fusion.1 = bf16[640,9,128]{2,1,0:T(8,128)(2,1)S(1)} fusion(bf16[1024,9,128]{2,1,0:T(8,128)(2,1)} %copy.24, s32[1024]{0:T(1024)S(1)} %pad_clamp_fusion.2), kind=kCustom, calls=%fused_computation.clone | custom fusion | bytes 2951680 | tf_op jit(solution)/shard_map/jit(_take)/gather | solution.py:109
  31.5 2.3 broadcast_select_fusion.1
  33.9 1.6 copy.25
  35.5 1.7 collective-permute-start
  37.2 3.5 %gather_fusion.2 = bf16[640,9,128]{2,1,0:T(8,128)(2,1)S(1)} fusion(bf16[1024,9,128]{2,1,0:T(8,128)(2,1)} %copy.24, s32[1024]{0:T(1024)S(1)} %pad_clamp_fusion.1), kind=kCustom, calls=%fused_computation.2.clone | custom fusion | bytes 2951680 | tf_op jit(solution)/shard_map/jit(_take)/gather | solution.py:110
  40.8 2.3 broadcast_select_fusion
  43.1 1.5 copy.27
  44.6 3.9 %collective-permute-start.1 = (bf16[640,9,128]{2,0,1:T(8,128)(2,1)}, bf16[640,9,128]{2,0,1:T(8,128)(2,1)}, u32[]{:S(2)}, u32[]{:S(2)}) collective-permute-start(bf16[640,9,128]{2,0,1:T(8,128)(2,1)} %copy.27), channel_id=1, source_target_pairs={{0,30},{2,0},{4,2},{6,4},{8,6},{10,8},{12,10},{14,12},{16,14},{18,... | collective-permute-start | bytes 4423688 | tf_op jit(solution)/shard_map/ppermute | solution.py:16
  51.4 49.8 %collective-permute-done = bf16[640,9,128]{2,0,1:T(8,128)(2,1)} collective-permute-done((bf16[640,9,128]{2,0,1:T(8,128)(2,1)}, bf16[640,9,128]{2,0,1:T(8,128)(2,1)}, u32[]{:S(2)}, u32[]{:S(2)}) %collective-permute-start) | collective-permute-done | bytes 1474592 | tf_op jit(solution)/shard_map/ppermute | solution.py:16
  101.1 1.9 collective-permute-done.1
  103.1 2.7 pad_maximum_fusion
  105.7 26.3 %copy.28 = bf16[2304,9,128]{2,1,0:T(8,128)(2,1)} copy(bf16[2304,9,128]{2,0,1:T(8,128)(2,1)S(1)} %pad_maximum_fusion) | data formatting | bytes 10616832
  132.0 2.5 broadcast_in_dim.28
  134.6 94.3 %while.11 = (s32[]{:T(128)}, f32[1024,1152]{1,0:T(8,128)}, s32[]{:T(128)}, s32[2560]{0:T(1024)}, f32[35,2560]{1,0:T(8,128)}, /*index=5*/s32[2560]{0:T(1024)}, bf...) while((s32[]{:T(128)}, f32[1024,1152]{1,0:T(8,128)}, ...), condition=%wide.region_1.3_spmd.clone, body=%wide.region_0.0_spmd.clone.sunk | while | flops 1713313280 | bytes 65880160 | solution.py:99
  135.4 4.9 %gather_fusion = bf16[512,9,128]{2,1,0:T(8,128)(2,1)S(1)} fusion(bf16[2304,9,128]{2,1,0:T(8,128)(2,1)} %get-tuple-element.505, s32[1024]{0:T(1024)S(1)} %pad_clamp_fusion.4), kind=kCustom, calls=%fused_computation.1.clone.clone.1 | custom fusion | bytes 2361344 | tf_op jit(solution)/shard_map/while/body/jit(_take)/gather | solution.py:121
  140.2 1.5 copy.35
  141.9 1.4 fusion.75
  144.0 1.3 fusion.77
  148.6 0.8 add_dynamic-update-slice_fusion.36
  149.4 0.8 add_dynamic-update-slice_fusion.37
  151.1 0.9 add_dynamic-update-slice_fusion.39
  152.0 0.9 constant_dynamic-slice_fusion.3
  153.1 2.0 multiply_convert_fusion.3
  159.7 6.3 %convolution_add_fusion.2 = f32[1024,1152]{1,0:T(8,128)} fusion(f32[1024,1152]{1,0:T(8,128)} %get-tuple-element.450, bf16[512,1152]{0,1:T(8,128)(2,1)S(1)} %fusion.88, s32[512]{0:T(512)S(1)} %dynamic_slice.26), kind=kOutput, calls=%fused_computation.4.clone.1 | convolution fusion | flops 1210187776 | bytes 10618880 | tf_op jit(solution)/shard_map/while/body/dot_general | solution.py:81
  166.8 4.9 %gather_fusion = bf16[512,9,128]{2,1,0:T(8,128)(2,1)S(1)} fusion(bf16[2304,9,128]{2,1,0:T(8,128)(2,1)} %get-tuple-element.505, s32[1024]{0:T(1024)S(1)} %pad_clamp_fusion.4), kind=kCustom, calls=%fused_computation.1.clone.clone.1 | custom fusion | bytes 2361344 | tf_op jit(solution)/shard_map/while/body/jit(_take)/gather | solution.py:121
  171.7 1.5 copy.35
  173.3 1.4 fusion.75
  175.4 1.3 fusion.77
  180.0 0.8 add_dynamic-update-slice_fusion.36
  182.5 0.9 add_dynamic-update-slice_fusion.39
  183.4 0.9 constant_dynamic-slice_fusion.3
  184.5 2.0 multiply_convert_fusion.3
  191.1 6.3 %convolution_add_fusion.2 = f32[1024,1152]{1,0:T(8,128)} fusion(f32[1024,1152]{1,0:T(8,128)} %get-tuple-element.450, bf16[512,1152]{0,1:T(8,128)(2,1)S(1)} %fusion.88, s32[512]{0:T(512)S(1)} %dynamic_slice.26), kind=kOutput, calls=%fused_computation.4.clone.1 | convolution fusion | flops 1210187776 | bytes 10618880 | tf_op jit(solution)/shard_map/while/body/dot_general | solution.py:81
  198.2 4.9 %gather_fusion = bf16[512,9,128]{2,1,0:T(8,128)(2,1)S(1)} fusion(bf16[2304,9,128]{2,1,0:T(8,128)(2,1)} %get-tuple-element.505, s32[1024]{0:T(1024)S(1)} %pad_clamp_fusion.4), kind=kCustom, calls=%fused_computation.1.clone.clone.1 | custom fusion | bytes 2361344 | tf_op jit(solution)/shard_map/while/body/jit(_take)/gather | solution.py:121
  203.1 1.5 copy.35
  204.7 1.4 fusion.75
  206.9 1.3 fusion.77
  211.4 0.8 add_dynamic-update-slice_fusion.36
  214.0 0.9 add_dynamic-update-slice_fusion.39
  214.8 0.9 constant_dynamic-slice_fusion.3
  215.9 2.0 multiply_convert_fusion.3
  222.5 6.3 %convolution_add_fusion.2 = f32[1024,1152]{1,0:T(8,128)} fusion(f32[1024,1152]{1,0:T(8,128)} %get-tuple-element.450, bf16[512,1152]{0,1:T(8,128)(2,1)S(1)} %fusion.88, s32[512]{0:T(512)S(1)} %dynamic_slice.26), kind=kOutput, calls=%fused_computation.4.clone.1 | convolution fusion | flops 1210187776 | bytes 10618880 | tf_op jit(solution)/shard_map/while/body/dot_general | solution.py:81
  228.9 6.1 %copy.30 = f32[1024,1152]{0,1:T(8,128)} copy(f32[1024,1152]{1,0:T(8,128)} %get-tuple-element.74) | data formatting | bytes 9437184 | tf_op jit(solution)/shard_map/while | solution.py:99
  234.9 75.5 %reduce-scatter.2.cloned.1.call-done = f32[512,1152]{0,1:T(8,128)} async-done(((f32[1024,1152]{0,1:T(8,128)}), f32[512,1152]{0,1:T(8,128)}) %reduce-scatter.2.cloned.1.call-update) | async-done | bytes 2359312 | tf_op jit(solution)/shard_map/reduce_scatter | solution.py:126
  310.4 2.0 multiply_convert_fusion.1
  312.4 1.4 copy.31
  (152 shorter events, 36.3 us)
Async XLA Ops:
  6.5 16.1 %all-gather.2.cloned.1.call-start = ((), (), s32[]{:S(2)}) async-start(), calls=%async_computation.1 | async-start | bytes 3538944 | tf_op jit(solution)/shard_map/all_gather | solution.py:108
  7.3 303.2 %reduce-scatter.2.cloned.1.call-start = ((), (), s32[]{:S(2)}) async-start(), calls=%async_computation.2 | async-start | bytes 7077888 | tf_op jit(solution)/shard_map/reduce_scatter | solution.py:126
  35.5 65.7 %collective-permute-start = (bf16[640,9,128]{2,0,1:T(8,128)(2,1)}, bf16[640,9,128]{2,0,1:T(8,128)(2,1)}, u32[]{:S(2)}, u32[]{:S(2)}) collective-permute-start(bf16[640,9,128]{2,0,1:T(8,128)(2,1)} %copy.25), channel_id=1, source_target_pairs={{0,2},{2,4},{4,6},{6,8},{8,10},{10,12},{12,14},{14,16},{16,18},{18... | collective-permute-start | bytes 4423688 | tf_op jit(solution)/shard_map/ppermute | solution.py:16
  43.1 5.5 %copy-start.5 = (s32[16,2]{0,1:T(2,128)S(1)}, s32[16,2]{0,1:T(2,128)}, u32[]{:S(2)}) copy-start(s32[16,2]{0,1:T(2,128)} %param.18) | copy-start | bytes 388
  43.1 6.7 %copy-start.3 = (bf16[2,128,128]{2,1,0:T(8,128)(2,1)S(1)}, bf16[2,128,128]{2,1,0:T(8,128)(2,1)}, u32[]{:S(2)}) copy-start(bf16[2,128,128]{2,1,0:T(8,128)(2,1)} %param.23) | copy-start | bytes 196612
  43.1 7.4 %copy-start.1 = (bf16[2,256,256]{2,1,0:T(8,128)(2,1)S(1)}, bf16[2,256,256]{2,1,0:T(8,128)(2,1)}, u32[]{:S(2)}) copy-start(bf16[2,256,256]{2,1,0:T(8,128)(2,1)} %param.22) | copy-start | bytes 786436
  43.1 60.0 %copy-start = (bf16[1024,9,128]{2,0,1:T(8,128)(2,1)S(1)}, bf16[1024,9,128]{2,0,1:T(8,128)(2,1)}, u32[]{:S(2)}) copy-start(bf16[1024,9,128]{2,0,1:T(8,128)(2,1)} %all-gather.2.cloned.1.call-done) | copy-start | bytes 7077892
  44.6 58.4 %collective-permute-start.1 = (bf16[640,9,128]{2,0,1:T(8,128)(2,1)}, bf16[640,9,128]{2,0,1:T(8,128)(2,1)}, u32[]{:S(2)}, u32[]{:S(2)}) collective-permute-start(bf16[640,9,128]{2,0,1:T(8,128)(2,1)} %copy.27), channel_id=1, source_target_pairs={{0,30},{2,0},{4,2},{6,4},{8,6},{10,8},{12,10},{14,12},{16,14},{18,... | collective-permute-start | bytes 4423688 | tf_op jit(solution)/shard_map/ppermute | solution.py:16
  153.0 2.2 copy-start.4
  155.1 1.0 copy-start.2
  155.2 1.4 copy-start.6
  184.5 2.2 copy-start.4
  186.5 1.0 copy-start.2
  186.7 1.4 copy-start.6
  215.9 2.2 copy-start.4
  217.9 1.0 copy-start.2
  218.1 1.4 copy-start.6
Sparse Core Ops, SparseCore 0:
  8.9 13.6 all-gather.1
  235.1 75.3 reduce-scatter.1
where the time goes:
time: 323 us; the launch traced here: 321 us
  waiting for transfers between devices  142 us (44%)
  local copies, waits for them, and re-layouts  88.4 us (27%)
  other arithmetic  46.8 us (14%)
  matrix products  22.4 us (7%)
  between operations  14.2 us (4%)
  starting transfers between devices  5.67 us (2%)
    reduce_scatter x1, waiting for transfers between devices, per_device(): lax.psum_scatter(partial_value, 'graph', scatter_dimension=0, tiled=True)  75.5 us
    ppermute x2, waiting for transfers between devices, shifted(): return lax.ppermute(x, axis, [(i, (i + by) % size) for i in range(size)])  51.7 us
    unnamed x9, local copies, waits for them, and re-layouts  26.3 us
    while x48, other arithmetic  22 us
    gather x6, local copies, waits for them, and re-layouts, local_mixed(): turned = front(jnp.take(lookup, src_index, axis=0), wig_rows, rad_rows)  19 us
    dot_general x3, matrix products, scatter_rows(): lax.dot_general(onehot, flat, (((0,), (0,)), ((), ())), preferred_element...  18.9 us
    all_gather x1, waiting for transfers between devices, per_device(): slab_rows = lax.all_gather(nodes, 'graph', axis=0, tiled=True)  14.5 us
    slice x6, local copies, waits for them, and re-layouts, rotate(): wig_rows[entry_index][:, None] * coeffs[:, first_coef + col_index, :]  8.19 us
  transfers between devices with their start and end apart: 4, of which 4 were waited for; matrix products, arithmetic and copies ran while one was open for 3% of the time, Pallas kernels for 0%

commit v1 on v0

v1 whole, which is shorter than its diff:
```python
import functools

import jax
import jax.numpy as jnp
from jax import lax
from jax.experimental import pallas as pl
from jax.experimental.pallas import tpu as pltpu
from jax.sharding import PartitionSpec as P

EDGE_BLOCK = 128
BLK = 256
LANES = 128
LAST_CHUNK = 256
STRIDE = 1 << 16
MESSAGE_SCALE = 0.2
WIGNER_BLOCKS = ((0, 0, 1), (1, 1, 3), (10, 4, 5))
ORDER = (0, 2, 6, 3, 7, 1, 5, 8, 4)
AXES = ("slab", "graph")
WROWS = 48
HI, LO, IDX, FEATS = 128, 176, 224, 256
VMEM_LIMIT = 56 * 1024 * 1024

f32, bf16, i32 = jnp.float32, jnp.bfloat16, jnp.int32


def nn(a, b):
    return lax.dot_general(a, b, (((1,), (0,)), ((), ())), preferred_element_type=f32)


def nt(a, b):
    return lax.dot_general(a, b, (((1,), (1,)), ((), ())), preferred_element_type=f32)


def hot(index, rows):
    return jnp.where(
        lax.broadcasted_iota(i32, (rows, index.shape[1]), 0) == index, 1.0, 0.0
    ).astype(bf16)


def call(body, out_shape, *args, smem=(), smem_out=(), scratch=(), flops=0, aliases=None):
    outs = out_shape if isinstance(out_shape, (tuple, list)) else (out_shape,)
    spec = lambda on: pl.BlockSpec(memory_space=pltpu.SMEM if on else pltpu.VMEM)
    size = sum(a.size * a.dtype.itemsize for a in (*args, *outs))
    return pl.pallas_call(
        body,
        out_shape=out_shape,
        in_specs=[spec(i in smem) for i in range(len(args))],
        out_specs=[spec(i in smem_out) for i in range(len(outs))]
        if isinstance(out_shape, (tuple, list))
        else spec(0 in smem_out),
        scratch_shapes=list(scratch),
        input_output_aliases=aliases or {},
        compiler_params=pltpu.CompilerParams(vmem_limit_bytes=VMEM_LIMIT),
        cost_estimate=pl.CostEstimate(flops=flops, bytes_accessed=size, transcendentals=0),
    )(*args)


def pack_first(own, sib, index, table, face):
    half = own.shape[1]
    for c in range(own.shape[0]):
        rows = slice(c * LANES, (c + 1) * LANES)
        for i in range(0, half, LANES):
            table[rows, i : i + LANES] = own[c, i : i + LANES, :].T
            table[rows, half + i : half + i + LANES] = sib[c, i : i + LANES, :].T
    face[...] = nn(table[...], hot(index[...], 2 * half)).astype(bf16)


def pack_next(table, index, face):
    face[...] = nn(table[...], hot(index[...], table.shape[1])).astype(bf16)


def features(radial, wigner, sources, targets, w_zero, w_one, w_two, feats, wz, w1, w2, padded):
    edges = radial.shape[0]
    for i in range(0, edges, LANES):
        feats[0:LANES, i : i + LANES] = radial[i : i + LANES, :].T
    padded[...] = jnp.zeros(padded.shape, f32)
    padded[0 : wigner.shape[0], :] = wigner[...]
    value = padded[...]
    high = value.astype(bf16)
    feats[HI:LO, :] = high
    feats[LO:IDX, :] = (value - high.astype(f32)).astype(bf16)
    row = lax.broadcasted_iota(i32, (FEATS - IDX, edges), 0)
    src, tgt = sources[...], targets[...]
    digits = jnp.where(row == 0, src // 256, jnp.where(row == 1, src % 256, 0))
    digits = jnp.where(row == 2, tgt // 256, jnp.where(row == 3, tgt % 256, digits))
    feats[IDX:FEATS, :] = digits.astype(f32).astype(bf16)
    wz[...] = w_zero[...].T
    for weights, out in ((w_one, w1), (w_two, w2)):
        n = weights.shape[1]
        real, imag = weights[0].T, weights[1].T
        out[0:n, 0:n] = real
        out[0:n, n : 2 * n] = (-imag.astype(f32)).astype(bf16)
        out[n : 2 * n, 0:n] = imag
        out[n : 2 * n, n : 2 * n] = real


def places(slab, face, first, info, own, sib, pos_own, pos_sib, counts):
    g = info[0]
    rows = own.shape[0]
    at_zero = g == 0
    parts = []
    for which in range(2):
        src = jnp.where(at_zero == (which == 0), own[...], sib[...])
        edge = lax.broadcasted_iota(i32, (rows, LANES), 0) * LANES + lax.broadcasted_iota(
            i32, (rows, LANES), 1
        )
        parts.append(jnp.where(edge < info[1 + which] * EDGE_BLOCK, src, -1))
    src = jnp.concatenate(parts, axis=0)
    at = src - slab - face * g
    on_face = jnp.logical_and(src >= slab, jnp.logical_and(at >= 0, at < face))
    masks = (
        jnp.logical_and(src >= 0, src < slab),
        jnp.logical_and(on_face, at < first),
        jnp.logical_and(on_face, at >= first),
    )
    both = 2 * rows
    upper = (
        lax.broadcasted_iota(i32, (LANES, LANES), 0) < lax.broadcasted_iota(i32, (LANES, LANES), 1)
    ).astype(f32).astype(bf16)
    lower = (
        lax.broadcasted_iota(i32, (both, both), 1) < lax.broadcasted_iota(i32, (both, both), 0)
    ).astype(f32).astype(bf16)
    ones = jnp.ones((LANES, LANES), bf16)
    pos = jnp.full((both, LANES), -1, i32)
    for k, mask in enumerate(masks):
        member = mask.astype(f32)
        m16 = member.astype(bf16)
        before = nn(nn(lower, m16).astype(bf16), ones) + nn(m16, upper)
        pos = jnp.where(mask, before.astype(i32) + k * STRIDE, pos)
        counts[k] = jnp.sum(member).astype(i32)
    low, high = pos[0:rows], pos[rows:both]
    pos_own[...] = jnp.where(at_zero, low, high)
    pos_sib[...] = jnp.where(at_zero, high, low)


def blocks_of(info, counts):
    total = [(counts[k] + (BLK - 1)) // BLK for k in range(3)]
    mine = (total[0] + 1 - info[0]) // 2
    return mine, total[1], total[2]


def group(info, counts, feat_own, feat_sib, pos_own, pos_sib, out, hot_own, hot_sib):
    n0, n1, n2 = blocks_of(info, counts)
    g = info[0]

    def step(t, carry):
        base = jnp.where(
            t < n0,
            (2 * t + g) * BLK,
            jnp.where(t < n0 + n1, STRIDE + (t - n0) * BLK, 2 * STRIDE + (t - n0 - n1) * BLK),
        )
        want = lax.broadcasted_iota(i32, (BLK, LANES), 0) + base
        for pos, mask in ((pos_own, hot_own), (pos_sib, hot_sib)):
            for i in range(pos.shape[0]):
                mask[:, i * LANES : (i + 1) * LANES] = jnp.where(
                    pos[i : i + 1, :] == want, 1.0, 0.0
                ).astype(bf16)
        picked = nt(feat_own[...], hot_own[...]) + nt(feat_sib[...], hot_sib[...])
        out[t] = picked.astype(bf16)
        return carry

    lax.fori_loop(0, n0 + n1 + n2, step, 0)


def messages_of(kind, shift, info, counts, grouped, table, wz, w1, w2, acc, x, w, rot, mix, msg):
    n = blocks_of(info, counts)
    start = (0, n[0], n[0] + n[1])[kind]
    g = info[0]
    slab = acc.shape[0]
    half = slab // 2
    rows = table.shape[1]
    n_zero, n_one, n_two = wz.shape[0], w1.shape[0], w2.shape[0]
    slot = {c: i for i, c in enumerate(ORDER)}

    def one(b, carry):
        at = start + b
        w[...] = grouped[at, HI:LO, :].astype(f32) + grouped[at, LO:IDX, :].astype(f32)
        digits = grouped[at, IDX : IDX + 16, :].astype(f32)
        src = (digits[0:1] * 256.0 + digits[1:2]).astype(i32)
        tgt = (digits[2:3] * 256.0 + digits[3:4]).astype(i32)
        if kind == 0:
            src = src + half * g
            src = jnp.where(src >= slab, src - slab, src)
        else:
            src = src - shift(g)
        tgt = tgt + half * g
        tgt = jnp.where(tgt >= slab, tgt - slab, tgt)
        x[...] = nn(table[...], hot(src, rows))
        for q in range(0, LANES, 16):
            rad = grouped[at, q : q + 16, :].astype(f32)
            for offset, first, size in WIGNER_BLOCKS:
                for i in range(size):
                    total = None
                    for j in range(size):
                        k = offset + i * size + j
                        r = (first + j) * LANES + q
                        term = w[k : k + 1, :] * x[r : r + 16, :]
                        total = term if total is None else total + term
                    r = slot[first + i] * LANES + q
                    rot[r : r + 16, :] = (total * rad).astype(bf16)
        mix[0:n_zero, :] = nn(wz[...], rot[0:n_zero, :])
        mix[n_zero : n_zero + n_one, :] = nn(w1[...], rot[n_zero : n_zero + n_one, :])
        mix[n_zero + n_one :, :] = nn(w2[...], rot[n_zero + n_one :, :])
        for q in range(0, LANES, 16):
            for offset, first, size in WIGNER_BLOCKS:
                for i in range(size):
                    total = None
                    for j in range(size):
                        k = offset + j * size + i
                        r = slot[first + j] * LANES + q
                        term = w[k : k + 1, :] * mix[r : r + 16, :]
                        total = term if total is None else total + term
                    r = (first + i) * LANES + q
                    msg[r : r + 16, :] = total.astype(bf16)
        acc[...] += nt(hot(tgt, slab), msg[...])
        return carry

    lax.fori_loop(0, n[kind], one, 0)


def sum_slab(info, counts, grouped, table, wz, w1, w2, acc, *scratch):
    acc[...] = jnp.zeros(acc.shape, f32)
    messages_of(0, None, info, counts, grouped, table, wz, w1, w2, acc, *scratch)


def sum_face(shift, info, counts, grouped, table, wz, w1, w2, before, acc, *scratch):
    acc[...] = before[...]
    messages_of(1, shift, info, counts, grouped, table, wz, w1, w2, acc, *scratch)


def sum_last(shift, info, counts, grouped, table, wz, w1, w2, before, own, send, acc, *scratch):
    acc[...] = before[...]
    messages_of(2, shift, info, counts, grouped, table, wz, w1, w2, acc, *scratch)
    half = own.shape[1]
    for c in range(own.shape[0]):
        columns = slice(c * LANES, (c + 1) * LANES)
        own[c] = acc[0:half, columns]
        send[c] = acc[half : 2 * half, columns].astype(bf16)


def per_device(
    nodes, boundary, sources, targets, block_counts, wigner, radial, w_zero, w_one, w_two
):
    half, coefs, chan = nodes.shape
    slab, width = 2 * half, coefs * chan
    face = boundary.shape[2]
    last = min(LAST_CHUNK, face // 2)
    first = face - last
    edges = sources.shape[0]
    n_slab = lax.axis_size("slab")
    s, g = lax.axis_index("slab"), lax.axis_index("graph")
    sds = jax.ShapeDtypeStruct

    place = lambda i, j: (i % n_slab) * 2 + j
    swap = [(place(i, j), place(i, 1 - j)) for i in range(n_slab) for j in range(2)]
    ring = [(place(i, 0), place(i + 1, 0)) for i in range(n_slab)]
    ring += [(place(i, 1), place(i - 1, 1)) for i in range(n_slab)]
    send = lambda x, to: lax.ppermute(x, AXES, to)

    own = jnp.transpose(nodes, (1, 0, 2))
    sib = send(own, swap)
    sources_own = sources.reshape(-1, LANES)
    sources_sib = send(sources_own, swap)
    info = jnp.concatenate([jnp.stack([g.astype(i32)]), lax.dynamic_index_in_dim(block_counts, s, 0, False)])

    listed = lax.dynamic_index_in_dim(boundary[0], 1 - g, 0, True)
    listed = listed + half * g
    listed = jnp.where(listed >= slab, listed - slab, listed)

    feats, wz, w1, w2 = call(
        features,
        (
            sds((FEATS, edges), bf16),
            sds(w_zero.shape, bf16),
            sds((2 * w_one.shape[1],) * 2, bf16),
            sds((2 * w_two.shape[1],) * 2, bf16),
        ),
        radial, wigner, sources[None], targets[None], w_zero, w_one, w_two,
        scratch=[pltpu.VMEM((WROWS, edges), f32)],
    )
    feats_sib = send(feats, swap)

    table, face_first = call(
        pack_first,
        (sds((width, slab), bf16), sds((width, first), bf16)),
        own, sib, listed[:, :first],
        flops=2 * width * slab * first,
    )
    got_first = send(face_first, ring)
    face_last = call(
        pack_next, sds((width, last), bf16), table, listed[:, first:], flops=2 * width * slab * last
    )
    got_last = send(face_last, ring)

    pos_own, pos_sib, counts = call(
        functools.partial(places, slab, face, first),
        (sds(sources_own.shape, i32), sds(sources_own.shape, i32), sds((3,), i32)),
        info, sources_own, sources_sib,
        smem=(0,), smem_out=(2,),
    )
    n_blocks = (2 * edges + BLK - 1) // BLK + 3
    grouped = call(
        group,
        sds((n_blocks, FEATS, BLK), bf16),
        info, counts, feats, feats_sib, pos_own, pos_sib,
        smem=(0, 1),
        scratch=[pltpu.VMEM((BLK, edges), bf16)] * 2,
        flops=2 * FEATS * BLK * edges * n_blocks,
    )

    scratch = [
        pltpu.VMEM((width, BLK), f32),
        pltpu.VMEM((WROWS, BLK), f32),
        pltpu.VMEM((width, BLK), bf16),
        pltpu.VMEM((width, BLK), f32),
        pltpu.VMEM((width, BLK), bf16),
    ]
    acc = call(
        sum_slab,
        sds((slab, width), f32),
        info, counts, grouped, table, wz, w1, w2,
        smem=(0, 1), scratch=scratch, flops=10 * 2 * BLK * width * (2 * slab + 512),
    )
    acc = call(
        functools.partial(sum_face, lambda g: slab + face * g),
        sds((slab, width), f32),
        info, counts, grouped, got_first, wz, w1, w2, acc,
        smem=(0, 1), scratch=scratch, flops=6 * 2 * BLK * width * (slab + 1024), aliases={7: 0},
    )
    mine, theirs = call(
        functools.partial(sum_last, lambda g: slab + face * g + first),
        (sds((coefs, half, chan), f32), sds((coefs, half, chan), bf16)),
        info, counts, grouped, got_last, wz, w1, w2, acc,
        smem=(0, 1), scratch=[pltpu.VMEM((slab, width), f32)] + scratch,
        flops=4 * 2 * BLK * width * (slab + 1024),
    )
    total = mine + send(theirs, swap).astype(f32)
    return jnp.transpose((total * MESSAGE_SCALE).astype(bf16), (1, 0, 2))


def solution(mesh):
    both = P(AXES)
    return jax.shard_map(
        per_device,
        mesh=mesh,
        in_specs=(
            P(AXES, None, None),
            P("slab", None, None),
            both,
            both,
            P(),
            P(None, AXES),
            P(AXES, None),
            P(),
            P(),
            P(),
        ),
        out_specs=P(AXES, None, None),
        check_vma=False,
    )
```

time: 323 us -> 98.1 us (0.30)
  the two profiles are of different devices: /device:TPU:0 before, /device:TPU:3 now
where the time goes in v1:
time: 98.1 us; the launch traced here: 97.7 us
  Pallas kernels  70.5 us (72%)
  starting transfers between devices  11.6 us (12%)
  local copies, waits for them, and re-layouts  8.4 us (9%)
  other arithmetic  4.29 us (4%)
  waiting for transfers between devices  2.82 us (3%)
    pallas_call x8, Pallas kernels, call(): pl.pallas_call(body, out_shape=out_shape, in_specs=[spec(i in smem) for i...  70.5 us
    ppermute x6, starting transfers between devices, per_device(): send = lambda x, to: lax.ppermute(x, AXES, to)  11.6 us
    unnamed x14, local copies, waits for them, and re-layouts  4.43 us
    transpose x1, other arithmetic, per_device(): return jnp.transpose((total * MESSAGE_SCALE).astype(bf16), (1, 0, 2))  3.01 us
    ppermute x6, waiting for transfers between devices, per_device(): send = lambda x, to: lax.ppermute(x, AXES, to)  2.82 us
  transfers between devices with their start and end apart: 6, of which 2 were waited for; matrix products, arithmetic and copies ran while one was open for 5% of the time, Pallas kernels for 61%

profile of v1, /device:TPU:3, one launch (start us, length us, event | category | flops | bytes accessed | tf_op | source)
XLA Modules:
  0.0 97.7 jit_solution(6557686548297979652)
XLA Ops:
  0.0 0.0 copy-start
  0.0 0.7 collective-permute-start.2
  0.7 1.3 %broadcast_in_dim.7.targets = s32[1,2560]{1,0:T(1,128)} reshape(s32[2560]{0:T(1024)} %param.13) | data formatting | bytes 20480 | tf_op jit(solution)/shard_map/broadcast_in_dim | solution.py:278
  2.0 1.3 %broadcast_in_dim.6.sources = s32[1,2560]{1,0:T(1,128)} reshape(s32[2560]{0:T(1024)} %param.12) | data formatting | bytes 20480 | tf_op jit(solution)/shard_map/broadcast_in_dim | solution.py:278
  3.3 3.1 %shard_map.101 = (bf16[256,2560]{1,0:T(8,128)(2,1)}, bf16[384,384]{1,0:T(8,128)(2,1)}, bf16[512,512]{1,0:T(8,128)(2,1)}, bf16[256,256]{1,0:T(8,128)(2,1)}) custom-call(bf16[2560,128]{1,0:T(8,128)(2,1)} %radial.1, f32[35,2560]{1,0:T(8,128)} %wigner.1, s32[1,2560]{1,0:T(1,128)} %broadcast_in_dim.6.sources, s32[1,2560]{1,0:T(1,128)} %broadcast_in_dim.7.targets, ...), custom_call_target="tpu_custom_call" | custom-call | bytes 3917824 | tf_op jit(solution)/shard_map/pallas_call | solution.py:44
  6.4 0.0 collective-permute-start.1
  6.4 0.5 collective-permute-start
  6.9 0.0 copy-done
  6.9 0.2 dynamic-slice_reduce_fusion
  7.1 0.7 compare_select_fusion
  7.8 0.6 pad_add_fusion.info
  8.4 0.6 slice.9.index
  8.9 0.6 slice.8.index
  9.5 0.1 collective-permute-done.sib
  9.7 0.0 copy-start.1
  9.7 0.6 copy-done.1
  10.3 1.8 %shard_map.100 = (s32[20,128]{1,0:T(8,128)}, s32[20,128]{1,0:T(8,128)}, s32[3]{0:T(128)}) custom-call(s32[3]{0:T(128)} %pad_add_fusion.info, s32[20,128]{1,0:T(8,128)} %bitcast.8, s32[20,128]{1,0:T(8,128)} %copy-done.1), custom_call_target="tpu_custom_call" | custom-call | bytes 40984 | tf_op jit(solution)/shard_map/pallas_call | solution.py:44
  12.0 0.0 collective-permute-done.2.sib
  12.0 0.0 copy-start.3
  12.1 1.0 %copy-done.3 = bf16[9,512,128]{2,1,0:T(8,128)(2,1)} copy-done((bf16[9,512,128]{2,1,0:T(8,128)(2,1)}, bf16[9,512,128]{2,1,0:T(8,128)(2,1)S(1)}, u32[]{:S(2)}) %copy-start.3) | copy-done | bytes 1179672
  13.1 4.6 %shard_map.103 = (bf16[1152,1024]{1,0:T(8,128)(2,1)}, bf16[1152,384]{1,0:T(8,128)(2,1)}) custom-call(bf16[9,512,128]{2,1,0:T(8,128)(2,1)} %bitcast.10, bf16[9,512,128]{2,1,0:T(8,128)(2,1)} %copy-done.3, s32[1,384]{1,0:T(1,128)} %slice.8.index), custom_call_target="tpu_custom_call" | custom-call | flops 905969664 | bytes 5604864 | tf_op jit(solution)/shard_map/pallas_call | solution.py:44
  17.7 0.0 copy-start.4
  17.7 3.4 %shard_map.104 = bf16[1152,256]{1,0:T(8,128)(2,1)} custom-call(bf16[1152,1024]{1,0:T(8,128)(2,1)} %get-tuple-element.20.table, s32[1,256]{1,0:T(1,128)} %slice.9.index), custom_call_target="tpu_custom_call" | custom-call | flops 603979776 | bytes 2950144 | tf_op jit(solution)/shard_map/pallas_call | solution.py:44
  21.1 0.0 collective-permute-start.3
  21.1 0.0 copy-done.4
  21.1 5.5 %collective-permute-start.4 = (bf16[1152,384]{1,0:T(8,128)(2,1)S(1)}, bf16[1152,384]{1,0:T(8,128)(2,1)S(1)}, u32[]{:S(2)}, u32[]{:S(2)}) collective-permute-start(bf16[1152,384]{1,0:T(8,128)(2,1)S(1)} %copy-done.4), channel_id=1, source_target_pairs={{0,2},{2,4},{4,6},{6,8},{8,10},{10,12},{12,14},{14,16},{16,18},{18... | collective-permute-start | bytes 2654216 | tf_op jit(solution)/shard_map/ppermute | solution.py:258
  26.5 0.0 collective-permute-done.1.feat_sib
  26.5 0.0 copy-start.2
  26.5 1.1 %copy-done.2 = bf16[256,2560]{1,0:T(8,128)(2,1)} copy-done((bf16[256,2560]{1,0:T(8,128)(2,1)}, bf16[256,2560]{1,0:T(8,128)(2,1)S(1)}, u32[]{:S(2)}) %copy-start.2) | copy-done | bytes 1310744
  27.6 12.6 %shard_map.102.grouped = bf16[23,256,256]{2,1,0:T(8,128)(2,1)} custom-call(s32[3]{0:T(128)} %pad_add_fusion.info, s32[3]{0:T(128)} %get-tuple-element.16.counts, bf16[256,2560]{1,0:T(8,128)(2,1)} %get-tuple-element.17.feat_own, bf16[256,2560]{1,0:T(8,128)(2,1)} %copy-done.2, s32[20,128]{1,0:T(8,128)} %get-tuple-element.18.pos_own, ...), custom_call_target="tpu_custom_call" | custom-call | flops 7717519360 | bytes 5656600 | tf_op jit(solution)/shard_map/pallas_call | solution.py:44
  40.2 18.4 %shard_map.105.before = f32[1024,1152]{1,0:T(8,128)} custom-call(s32[3]{0:T(128)} %pad_add_fusion.info, s32[3]{0:T(128)} %get-tuple-element.16.counts, bf16[23,256,256]{2,1,0:T(8,128)(2,1)} %shard_map.102.grouped, bf16[1152,1024]{1,0:T(8,128)(2,1)} %get-tuple-element.20.table, bf16[384,384]{1,0:T(8,128)(2,1)} %get-tuple-element.21.wz, ...), custom_call_target="tpu_custom_call" | custom-call | flops 15099494400 | bytes 11042840 | tf_op jit(solution)/shard_map/pallas_call | solution.py:44
  58.6 0.0 collective-permute-done.4.table
  58.6 0.0 copy-start.5
  58.6 0.9 copy-done.5
  59.5 16.2 %shard_map.106.before = f32[1024,1152]{1,0:T(8,128)} custom-call(s32[3]{0:T(128)} %pad_add_fusion.info, s32[3]{0:T(128)} %get-tuple-element.16.counts, bf16[23,256,256]{2,1,0:T(8,128)(2,1)} %shard_map.102.grouped, bf16[1152,384]{1,0:T(8,128)(2,1)} %copy-done.5, bf16[384,384]{1,0:T(8,128)(2,1)} %get-tuple-element.21.wz, ...), custom_call_target="tpu_custom_call", output_to_operand_aliasing={{}: (7, {})} | custom-call | flops 7247757312 | bytes 14286872 | tf_op jit(solution)/shard_map/pallas_call | solution.py:44
  75.7 0.0 collective-permute-done.3.table
  75.7 0.0 copy-start.6
  75.7 0.8 copy-done.6
  76.5 10.5 %shard_map.107 = (f32[9,512,128]{2,1,0:T(8,128)}, bf16[9,512,128]{2,1,0:T(8,128)(2,1)}) custom-call(s32[3]{0:T(128)} %pad_add_fusion.info, s32[3]{0:T(128)} %get-tuple-element.16.counts, bf16[23,256,256]{2,1,0:T(8,128)(2,1)} %shard_map.102.grouped, bf16[1152,256]{1,0:T(8,128)(2,1)} %copy-done.6, bf16[384,384]{1,0:T(8,128)(2,1)} %get-tuple-element.21.wz, ...), custom_call_target="tpu_custom_call" | custom-call | flops 4831838208 | bytes 12812312 | tf_op jit(solution)/shard_map/pallas_call | solution.py:44
  87.0 4.9 %collective-permute-start.5 = (bf16[9,512,128]{2,1,0:T(8,128)(2,1)}, bf16[9,512,128]{2,1,0:T(8,128)(2,1)S(1)}, u32[]{:S(2)}, u32[]{:S(2)}) collective-permute-start(bf16[9,512,128]{2,1,0:T(8,128)(2,1)} %get-tuple-element.26), channel_id=1, source_target_pairs={{0,1},{1,0},{2,3},{3,2},{4,5},{5,4},{6,7},{7,6},{8,9},{9,8},{10,11... | collective-permute-start | bytes 3538952 | tf_op jit(solution)/shard_map/ppermute | solution.py:258
  92.0 2.7 %collective-permute-done.5 = bf16[9,512,128]{2,1,0:T(8,128)(2,1)S(1)} collective-permute-done((bf16[9,512,128]{2,1,0:T(8,128)(2,1)}, bf16[9,512,128]{2,1,0:T(8,128)(2,1)S(1)}, u32[]{:S(2)}, u32[]{:S(2)}) %collective-permute-start.5) | collective-permute-done | bytes 1179680 | tf_op jit(solution)/shard_map/ppermute | solution.py:258
  94.6 3.0 %fusion = bf16[512,9,128]{2,0,1:T(8,128)(2,1)} fusion(f32[9,512,128]{2,1,0:T(8,128)} %get-tuple-element.25, bf16[9,512,128]{2,1,0:T(8,128)(2,1)S(1)} %collective-permute-done.5), kind=kLoop, calls=%fused_computation.1 | loop fusion | flops 2359296 | bytes 4718592 | tf_op jit(solution)/shard_map/transpose | solution.py:338
Async XLA Ops:
  0.0 6.9 %copy-start = (s32[16,2]{0,1:T(2,128)S(1)}, s32[16,2]{0,1:T(2,128)}, u32[]{:S(2)}) copy-start(s32[16,2]{0,1:T(2,128)} %param.14) | copy-start | bytes 388
  0.0 12.0 %collective-permute-start.2 = (bf16[9,512,128]{2,1,0:T(8,128)(2,1)}, bf16[9,512,128]{2,1,0:T(8,128)(2,1)S(1)}, u32[]{:S(2)}, u32[]{:S(2)}) collective-permute-start(bf16[9,512,128]{2,1,0:T(8,128)(2,1)} %bitcast.9), channel_id=1, source_target_pairs={{0,1},{1,0},{2,3},{3,2},{4,5},{5,4},{6,7},{7,6},{8,9},{9,8},{10,11... | collective-permute-start | bytes 3538952 | tf_op jit(solution)/shard_map/ppermute | solution.py:258
  6.4 20.1 %collective-permute-start.1 = (bf16[256,2560]{1,0:T(8,128)(2,1)}, bf16[256,2560]{1,0:T(8,128)(2,1)S(1)}, u32[]{:S(2)}, u32[]{:S(2)}) collective-permute-start(bf16[256,2560]{1,0:T(8,128)(2,1)} %get-tuple-element.17.feat_own), channel_id=1, source_target_pairs={{0,1},{1,0},{2,3},{3,2},{4,5},{5,4},{6,7},{7,6},{8,9},{9,8},{10,11... | collective-permute-start | bytes 3932168 | tf_op jit(solution)/shard_map/ppermute | solution.py:258
  6.4 3.3 %collective-permute-start = (s32[20,128]{1,0:T(8,128)}, s32[20,128]{1,0:T(8,128)S(1)}, u32[]{:S(2)}, u32[]{:S(2)}) collective-permute-start(s32[20,128]{1,0:T(8,128)} %bitcast.7), channel_id=1, source_target_pairs={{0,1},{1,0},{2,3},{3,2},{4,5},{5,4},{6,7},{7,6},{8,9},{9,8},{10,11... | collective-permute-start | bytes 30728 | tf_op jit(solution)/shard_map/ppermute | solution.py:258
  9.7 0.6 copy-start.1
  12.0 1.0 %copy-start.3 = (bf16[9,512,128]{2,1,0:T(8,128)(2,1)}, bf16[9,512,128]{2,1,0:T(8,128)(2,1)S(1)}, u32[]{:S(2)}) copy-start(bf16[9,512,128]{2,1,0:T(8,128)(2,1)S(1)} %collective-permute-done.2.sib) | copy-start | bytes 3538948
  17.7 3.4 %copy-start.4 = (bf16[1152,384]{1,0:T(8,128)(2,1)S(1)}, bf16[1152,384]{1,0:T(8,128)(2,1)}, u32[]{:S(2)}) copy-start(bf16[1152,384]{1,0:T(8,128)(2,1)} %get-tuple-element.24) | copy-start | bytes 2654212
  21.1 54.6 %collective-permute-start.3 = (bf16[1152,256]{1,0:T(8,128)(2,1)}, bf16[1152,256]{1,0:T(8,128)(2,1)S(1)}, u32[]{:S(2)}, u32[]{:S(2)}) collective-permute-start(bf16[1152,256]{1,0:T(8,128)(2,1)} %shard_map.104), channel_id=1, source_target_pairs={{0,2},{2,4},{4,6},{6,8},{8,10},{10,12},{12,14},{14,16},{16,18},{18... | collective-permute-start | bytes 1769480 | tf_op jit(solution)/shard_map/ppermute | solution.py:258
  21.1 37.5 %collective-permute-start.4 = (bf16[1152,384]{1,0:T(8,128)(2,1)S(1)}, bf16[1152,384]{1,0:T(8,128)(2,1)S(1)}, u32[]{:S(2)}, u32[]{:S(2)}) collective-permute-start(bf16[1152,384]{1,0:T(8,128)(2,1)S(1)} %copy-done.4), channel_id=1, source_target_pairs={{0,2},{2,4},{4,6},{6,8},{8,10},{10,12},{12,14},{14,16},{16,18},{18... | collective-permute-start | bytes 2654216 | tf_op jit(solution)/shard_map/ppermute | solution.py:258
  26.5 1.1 %copy-start.2 = (bf16[256,2560]{1,0:T(8,128)(2,1)}, bf16[256,2560]{1,0:T(8,128)(2,1)S(1)}, u32[]{:S(2)}) copy-start(bf16[256,2560]{1,0:T(8,128)(2,1)S(1)} %collective-permute-done.1.feat_sib) | copy-start | bytes 3932164
  58.6 0.9 copy-start.5
  75.7 0.8 copy-start.6
  87.0 7.6 %collective-permute-start.5 = (bf16[9,512,128]{2,1,0:T(8,128)(2,1)}, bf16[9,512,128]{2,1,0:T(8,128)(2,1)S(1)}, u32[]{:S(2)}, u32[]{:S(2)}) collective-permute-start(bf16[9,512,128]{2,1,0:T(8,128)(2,1)} %get-tuple-element.26), channel_id=1, source_target_pairs={{0,1},{1,0},{2,3},{3,2},{4,5},{5,4},{6,7},{7,6},{8,9},{9,8},{10,11... | collective-permute-start | bytes 3538952 | tf_op jit(solution)/shard_map/ppermute | solution.py:258
